TPU v7x, 512 devices: a whole 4x8x8 slice. The times are simulated.
512 devices in a mesh: blk: 32 (over y_hi, z, core), col: 16 (over y_lo, x).
Axes of the slice: x: 4, y: 8 (y_hi: 2, y_lo: 4; y = y_hi * 4 + y_lo), z: 8, core: 2. Of those that a mesh axis runs over, the one named last changes fastest.
Arguments:
- pair_rep: bfloat16 [512, 512, 128], P('blk', 'col'), may hold values from -6 to 6
- norm_gain: float32 [128], replicated, may hold values from 0.5 to 1.5
- norm_shift: float32 [128], replicated, may hold values from -3 to 3
- w_query: bfloat16 [128, 128], replicated, may hold values from -5 to 5
- w_key: bfloat16 [128, 128], replicated, may hold values from -5 to 5
- w_value: bfloat16 [128, 128], replicated, may hold values from -0.5 to 0.5
- w_bias: bfloat16 [128, 4], replicated, may hold values from -1.5 to 1.5
- w_gate: bfloat16 [128, 128], replicated, may hold values from -0.5 to 0.5
- gate_shift: float32 [128], replicated, may hold values from -4 to 4
- w_out: bfloat16 [128, 128], replicated, may hold values from -0.5 to 0.5
Outputs:
- update: bfloat16 [512, 512, 128], P('blk', 'col')
All inputs are finite; a program needn't handle non-finite values.
Results may differ from a plain program's by a relative error of at most 0.012.
The roundings to bfloat16 on the way count: a program that leaves them out, or rounds other values in their place, can miss the bound.
Values may be sent and summed in bfloat16 or wider, within the bound.
A program may use at most 128 MiB of HBM per device.

v0:
```python
import jax
import jax.numpy as jnp
from jax import lax
from jax.sharding import PartitionSpec as P


def spread(x, axis, root):
    mine = lax.axis_index(axis) == root
    return lax.psum(jnp.where(mine, x, jnp.zeros_like(x)), axis)


def layer_norm(pair_rep, norm_gain, norm_shift):
    centered = pair_rep.astype(jnp.float32)
    average = jnp.mean(centered, axis=-1, keepdims=True)
    centered = centered - average
    variance = jnp.mean(centered * centered, axis=-1, keepdims=True)
    return (centered * lax.rsqrt(variance + 1e-05) * norm_gain + norm_shift).astype(jnp.bfloat16)


def block_length(count):
    divisor = min(count, 128)
    while count % divisor != 0:
        divisor = divisor - 1
    return divisor


def attend_block(running, queries, key_block, value_block, bias_block):
    run_max, run_total, run_acc = running
    scores = jnp.einsum("rjhd,pjhd->rjhp", queries, key_block, preferred_element_type=jnp.float32)
    scores = scores + bias_block[:, None, :, :]
    new_max = jnp.maximum(run_max, jnp.max(scores, axis=-1))
    rescale = jnp.exp(run_max - new_max)
    expo = jnp.exp(scores - new_max[..., None])
    new_total = run_total * rescale + jnp.sum(expo, axis=-1)
    weights = expo.astype(jnp.bfloat16)
    numerator = jnp.einsum(
        "rjhp,pjhd->rjhd", weights, value_block, preferred_element_type=jnp.float32
    )
    return (new_max, new_total, run_acc * rescale[..., None] + numerator)


def sweep(running, received, queries, bias_turned, make_pairs):
    count = received[0].shape[0]
    step_rows = block_length(count)
    steps_count = count // step_rows
    stacked = tuple((arr.reshape((steps_count, step_rows) + arr.shape[1:]) for arr in received))

    def advance(state, operands):
        position, blocks_in = (operands[0], operands[1:])
        key_block, value_block = make_pairs(blocks_in)
        bias_block = lax.dynamic_slice_in_dim(bias_turned, position * step_rows, step_rows, 2)
        return (attend_block(state, queries, key_block, value_block, bias_block), None)

    positions = jnp.arange(steps_count, dtype=jnp.int32)
    result, unused = lax.scan(advance, running, (positions,) + stacked)
    return result


def given_path(normed, own_bias, w_query, w_key, w_value, w_gate, gate_shift, w_out):
    row_count, col_count, channels = normed.shape
    head_count = own_bias.shape[2]
    head_size = channels // head_count
    flat_normed = normed.reshape(-1, channels)
    query_scale = 1.0 / head_size**0.5
    queries = (
        jnp.dot(flat_normed, w_query, preferred_element_type=jnp.float32) * query_scale
    ).astype(jnp.bfloat16)
    queries = queries.reshape(row_count, col_count, head_count, head_size)
    gating = jax.nn.sigmoid(
        jnp.dot(flat_normed, w_gate, preferred_element_type=jnp.float32) + gate_shift
    )
    row_block = lax.axis_index("blk")
    col_group = lax.axis_index("col")
    owner_group = row_block * row_count // col_count
    column_bias = lax.all_gather(own_bias, "blk", axis=0, tiled=True)
    offset = jnp.clip(row_block * row_count - col_group * col_count, 0, col_count - row_count)
    local_bias = lax.dynamic_slice_in_dim(column_bias, offset, row_count, 1)
    needed = spread(local_bias, "col", owner_group)
    bias_turned = needed.astype(jnp.float32).transpose(1, 2, 0)
    initial = (
        jnp.full((row_count, col_count, head_count), -1e30, jnp.float32),
        jnp.zeros((row_count, col_count, head_count), jnp.float32),
        jnp.zeros((row_count, col_count, head_count, head_size), jnp.float32),
    )

    def project_pairs(blocks_in):
        slab = blocks_in[0]
        step_rows = slab.shape[0]
        flat_slab = slab.reshape(-1, channels)
        key_block = jnp.dot(flat_slab, w_key, preferred_element_type=jnp.float32).astype(
            jnp.bfloat16
        )
        value_block = jnp.dot(flat_slab, w_value, preferred_element_type=jnp.float32).astype(
            jnp.bfloat16
        )
        return (
            key_block.reshape(step_rows, col_count, head_count, head_size),
            value_block.reshape(step_rows, col_count, head_count, head_size),
        )

    final = sweep(
        initial,
        (lax.all_gather(normed, "blk", axis=0, tiled=True),),
        queries,
        bias_turned,
        project_pairs,
    )
    run_max, run_total, run_acc = final
    attended = (run_acc / run_total[..., None]).reshape(-1, channels)
    hidden = (gating * attended).astype(jnp.bfloat16)
    result = jnp.dot(hidden, w_out, preferred_element_type=jnp.float32).astype(jnp.bfloat16)
    return result.reshape(row_count, col_count, channels)


def per_device(
    pair_rep, norm_gain, norm_shift, w_query, w_key, w_value, w_bias, w_gate, gate_shift, w_out
):
    row_count, col_count, channels = pair_rep.shape
    head_count = w_bias.shape[1]
    normed = layer_norm(pair_rep, norm_gain, norm_shift)
    flat_normed = normed.reshape(-1, channels)
    own_bias = jnp.dot(flat_normed, w_bias, preferred_element_type=jnp.float32).astype(jnp.bfloat16)
    own_bias = own_bias.reshape(row_count, col_count, head_count)
    return given_path(normed, own_bias, w_query, w_key, w_value, w_gate, gate_shift, w_out)


def solution(mesh):
    placed = (P("blk", "col", None), P(), P(), P(), P(), P(), P(), P(), P(), P())
    return jax.shard_map(
        per_device, mesh=mesh, in_specs=placed, out_specs=P("blk", "col", None), check_vma=False
    )
```

profile of v0, /device:TPU:2, one launch (start us, length us, event | category | flops | bytes accessed | tf_op | source)
XLA Modules:
  0.0 363.4 jit_solution(3713048332932100053)
XLA Ops:
  7.4 1.0 convert_reduce_fusion
  8.5 1.2 fusion.30
  9.7 1.1 fusion.33
  10.8 0.8 convolution_convert_fusion.3
  11.8 61.7 %all_gather.7 = bf16[512,32,4]{1,2,0:T(4,128)(2,1)S(1)} all-gather(bf16[16,32,4]{1,2,0:T(4,128)(2,1)S(1)} %copy.26), channel_id=1, replica_groups=mesh['blk'=32,'col'=16] {'blk'}, dimensions={0}, use_global_device_ids=true | all-gather | bytes 135168 | tf_op jit(solution)/shard_map/all_gather | solution.py:75
  73.5 1.2 select_bitcast_fusion
  74.8 0.5 all-gather.2.cloned.1.call-update
  75.3 1.1 fusion.27
  76.7 1.4 copy.27
  78.1 172.8 %all-reduce.2.cloned.1.call-done = bf16[16,4,512]{0,1,2:T(4,128)(2,1)} async-done(((bf16[16,4,512]{0,1,2:T(4,128)(2,1)}), bf16[16,4,512]{0,1,2:T(4,128)(2,1)}) %all-reduce.2.cloned.1.call-update) | async-done | bytes 65552 | tf_op jit(solution)/shard_map/psum | solution.py:9
  250.9 2.0 copy.28
  253.0 99.4 %while.15 = (s32[]{:T(128)}, f32[16,32,4]{0,2,1:T(4,128)S(1)}, f32[16,32,4]{0,2,1:T(4,128)S(1)}, f32[16,32,4,32]{3,0,2,1:T(8,128)}, bf16[4,128,32,128]{3,2,1,0:T...) while((s32[]{:T(128)}, f32[16,32,4]{0,2,1:T(4,128)S(1)}, ...), condition=%wide.region_6.7_spmd.clone, body=%wide.region_3.6_spmd.clone.sunk | while | flops 304818176 | bytes 16679123 | solution.py:55
  253.2 0.6 dynamic_slice.26
  254.3 0.8 constant_dynamic-slice_fusion.4
  255.1 1.3 constant_dynamic-slice_fusion.5
  256.8 3.3 reshape.64
  260.1 6.0 %fusion.68 = (f32[16,32,4]{0,2,1:T(4,128)S(1)}, f32[16,32,4,128]{3,0,2,1:T(8,128)S(1)}) fusion(f32[16,4,128]{2,0,1:T(8,128)S(1)} %constant_dynamic-slice_fusion.4, bf16[16,32,4,32]{3,0,2,1:T(8,128)(2,1)} %get-tuple-element.250, bf16[128,32,4,32]{3,2,1,0:T(4,128)(2,1)} %reshape.64), kind=kOutput, calls=%fused_computation.47.clone.1 | convolution fusion | flops 17299456 | bytes 2269184 | tf_op jit(solution)/shard_map/while/body/eval_jaxpr/rjhd,pjhd->rjhp/dot_general | solution.py:29
  266.1 0.7 fusion.69
  267.3 3.3 reshape.65
  270.6 7.2 %fusion.71 = f32[16,32,4,32]{3,0,2,1:T(8,128)} fusion(bf16[128,32,4,32]{3,2,1,0:T(4,128)(2,1)} %reshape.65, f32[16,32,4,32]{3,0,2,1:T(8,128)} %get-tuple-element.233, f32[16,32,4,128]{3,0,2,1:T(8,128)S(1)} %get-tuple-element.213, f32[16,32,4]{0,2,1:T(4,128)S(1)} %get-tuple-element.215, f32[16,32,4]{0,2,1:T(4,128)S(1)} %select_maximum_fusion.2, ...), kind=kOutput, calls=%fused_computation.9.clone.1 | convolution fusion | flops 17498112 | bytes 2637825 | tf_op jit(solution)/shard_map/while/body/eval_jaxpr/rjhp,pjhd->rjhd/dot_general | solution.py:36
  277.7 0.6 dynamic_slice.26
  278.9 0.8 constant_dynamic-slice_fusion.4
  279.6 1.3 constant_dynamic-slice_fusion.5
  281.4 3.3 reshape.64
  284.6 6.0 %fusion.68 = (f32[16,32,4]{0,2,1:T(4,128)S(1)}, f32[16,32,4,128]{3,0,2,1:T(8,128)S(1)}) fusion(f32[16,4,128]{2,0,1:T(8,128)S(1)} %constant_dynamic-slice_fusion.4, bf16[16,32,4,32]{3,0,2,1:T(8,128)(2,1)} %get-tuple-element.250, bf16[128,32,4,32]{3,2,1,0:T(4,128)(2,1)} %reshape.64), kind=kOutput, calls=%fused_computation.47.clone.1 | convolution fusion | flops 17299456 | bytes 2269184 | tf_op jit(solution)/shard_map/while/body/eval_jaxpr/rjhd,pjhd->rjhp/dot_general | solution.py:29
  290.6 0.7 fusion.69
  291.9 3.3 reshape.65
  295.1 7.5 %fusion.71 = f32[16,32,4,32]{3,0,2,1:T(8,128)} fusion(bf16[128,32,4,32]{3,2,1,0:T(4,128)(2,1)} %reshape.65, f32[16,32,4,32]{3,0,2,1:T(8,128)} %get-tuple-element.233, f32[16,32,4,128]{3,0,2,1:T(8,128)S(1)} %get-tuple-element.213, f32[16,32,4]{0,2,1:T(4,128)S(1)} %get-tuple-element.215, f32[16,32,4]{0,2,1:T(4,128)S(1)} %select_maximum_fusion.2, ...), kind=kOutput, calls=%fused_computation.9.clone.1 | convolution fusion | flops 17498112 | bytes 2637825 | tf_op jit(solution)/shard_map/while/body/eval_jaxpr/rjhp,pjhd->rjhd/dot_general | solution.py:36
  302.6 0.6 dynamic_slice.26
  303.7 0.8 constant_dynamic-slice_fusion.4
  304.5 1.3 constant_dynamic-slice_fusion.5
  306.2 3.3 reshape.64
  309.5 6.0 %fusion.68 = (f32[16,32,4]{0,2,1:T(4,128)S(1)}, f32[16,32,4,128]{3,0,2,1:T(8,128)S(1)}) fusion(f32[16,4,128]{2,0,1:T(8,128)S(1)} %constant_dynamic-slice_fusion.4, bf16[16,32,4,32]{3,0,2,1:T(8,128)(2,1)} %get-tuple-element.250, bf16[128,32,4,32]{3,2,1,0:T(4,128)(2,1)} %reshape.64), kind=kOutput, calls=%fused_computation.47.clone.1 | convolution fusion | flops 17299456 | bytes 2269184 | tf_op jit(solution)/shard_map/while/body/eval_jaxpr/rjhd,pjhd->rjhp/dot_general | solution.py:29
  315.5 0.7 fusion.69
  316.3 0.4 convolution_convert_fusion.7
  316.7 3.3 reshape.65
  320.0 7.5 %fusion.71 = f32[16,32,4,32]{3,0,2,1:T(8,128)} fusion(bf16[128,32,4,32]{3,2,1,0:T(4,128)(2,1)} %reshape.65, f32[16,32,4,32]{3,0,2,1:T(8,128)} %get-tuple-element.233, f32[16,32,4,128]{3,0,2,1:T(8,128)S(1)} %get-tuple-element.213, f32[16,32,4]{0,2,1:T(4,128)S(1)} %get-tuple-element.215, f32[16,32,4]{0,2,1:T(4,128)S(1)} %select_maximum_fusion.2, ...), kind=kOutput, calls=%fused_computation.9.clone.1 | convolution fusion | flops 17498112 | bytes 2637825 | tf_op jit(solution)/shard_map/while/body/eval_jaxpr/rjhp,pjhd->rjhd/dot_general | solution.py:36
  327.5 0.6 dynamic_slice.26
  328.6 0.8 constant_dynamic-slice_fusion.4
  329.4 1.3 constant_dynamic-slice_fusion.5
  331.1 3.3 reshape.64
  334.3 6.0 %fusion.68 = (f32[16,32,4]{0,2,1:T(4,128)S(1)}, f32[16,32,4,128]{3,0,2,1:T(8,128)S(1)}) fusion(f32[16,4,128]{2,0,1:T(8,128)S(1)} %constant_dynamic-slice_fusion.4, bf16[16,32,4,32]{3,0,2,1:T(8,128)(2,1)} %get-tuple-element.250, bf16[128,32,4,32]{3,2,1,0:T(4,128)(2,1)} %reshape.64), kind=kOutput, calls=%fused_computation.47.clone.1 | convolution fusion | flops 17299456 | bytes 2269184 | tf_op jit(solution)/shard_map/while/body/eval_jaxpr/rjhd,pjhd->rjhp/dot_general | solution.py:29
  340.4 0.7 fusion.69
  341.6 3.3 reshape.65
  344.9 7.5 %fusion.71 = f32[16,32,4,32]{3,0,2,1:T(8,128)} fusion(bf16[128,32,4,32]{3,2,1,0:T(4,128)(2,1)} %reshape.65, f32[16,32,4,32]{3,0,2,1:T(8,128)} %get-tuple-element.233, f32[16,32,4,128]{3,0,2,1:T(8,128)S(1)} %get-tuple-element.213, f32[16,32,4]{0,2,1:T(4,128)S(1)} %get-tuple-element.215, f32[16,32,4]{0,2,1:T(4,128)S(1)} %select_maximum_fusion.2, ...), kind=kOutput, calls=%fused_computation.9.clone.1 | convolution fusion | flops 17498112 | bytes 2637825 | tf_op jit(solution)/shard_map/while/body/eval_jaxpr/rjhp,pjhd->rjhd/dot_general | solution.py:36
  352.4 1.6 broadcast_divide_fusion
  354.4 0.5 reshape.59
  354.9 1.0 convolution_convert_fusion.2
  (49 shorter events, 4.3 us)
Async XLA Ops:
  7.4 68.0 %copy-start = (bf16[128,128]{1,0:T(8,128)(2,1)S(1)}, bf16[128,128]{1,0:T(8,128)(2,1)}, u32[]{:S(2)}) copy-start(bf16[128,128]{1,0:T(8,128)(2,1)} %param.15) | copy-start | bytes 98308
  7.4 245.6 %copy-start.3 = (bf16[128,128]{1,0:T(8,128)(2,1)S(1)}, bf16[128,128]{1,0:T(8,128)(2,1)}, u32[]{:S(2)}) copy-start(bf16[128,128]{1,0:T(8,128)(2,1)} %param.16) | copy-start | bytes 98308
  7.4 245.6 %copy-start.4 = (bf16[128,128]{1,0:T(8,128)(2,1)S(1)}, bf16[128,128]{1,0:T(8,128)(2,1)}, u32[]{:S(2)}) copy-start(bf16[128,128]{1,0:T(8,128)(2,1)} %param.17) | copy-start | bytes 98308
  7.4 243.5 %all-reduce.2.cloned.1.call-start = ((), (), s32[]{:S(2)}) async-start(), calls=%async_computation.1 | async-start | bytes 1048576 | tf_op jit(solution)/shard_map/psum | solution.py:9
  10.8 64.0 %copy-start.1 = (bf16[16,32,128]{2,1,0:T(8,128)(2,1)}, bf16[16,32,128]{2,1,0:T(8,128)(2,1)S(1)}, u32[]{:S(2)}) copy-start(bf16[16,32,128]{2,1,0:T(8,128)(2,1)S(1)} %fusion.33) | copy-start | bytes 393220
  74.7 178.2 %all-gather.2.cloned.1.call-start = ((), (), s32[]{:S(2)}) async-start(), calls=%async_computation | async-start | bytes 4325376 | tf_op jit(solution)/shard_map/all_gather | solution.py:103
  352.3 2.6 copy-start.2
  352.3 2.6 copy-start.5
  352.3 2.6 copy-start.6
  352.4 2.6 copy-start.7
Sparse Core Ops, SparseCore 0:
  74.9 176.0 all-reduce.1
Sparse Core Ops, SparseCore 1:
  78.6 98.8 all-gather.1
where the time goes:
time: 364 us; the launch traced here: 363 us
  waiting for transfers between devices  173 us (48%)
  blocking collectives  61.7 us (17%)
  matrix products  59.7 us (16%)
  local copies, waits for them, and re-layouts  41.3 us (11%)
  between operations  15.1 us (4%)
  other arithmetic  9.52 us (3%)
    psum x1, waiting for transfers between devices, spread(): return lax.psum(jnp.where(mine, x, jnp.zeros_like(x)), axis)  173 us
    all_gather x1, blocking collectives, given_path(): column_bias = lax.all_gather(own_bias, 'blk', axis=0, tiled=True)  61.7 us
    dot_general x4, matrix products, attend_block(): jnp.einsum('rjhp,pjhd->rjhd', weights, value_block, preferred_element_typ...  29.5 us
    dot_general x4, matrix products, attend_block(): jnp.einsum('rjhd,pjhd->rjhp', queries, key_block, preferred_element_type=...  24 us
    reshape x4, local copies, waits for them, and re-layouts, project_pairs(): value_block.reshape(step_rows, col_count, head_count, head_size)  13 us
    reshape x4, local copies, waits for them, and re-layouts, project_pairs(): key_block.reshape(step_rows, col_count, head_count, head_size)  13 us
    dynamic_slice x8, local copies, waits for them, and re-layouts, sweep(): result, unused = lax.scan(advance, running, (positions,) + stacked)  7.47 us
  transfers between devices with their start and end apart: 2, of which 1 were waited for; matrix products, arithmetic and copies ran while one was open for 1% of the time, Pallas kernels for 0%

commit v1 on v0

v1 whole, which is shorter than its diff:
```python
import jax
import jax.numpy as jnp
from jax import lax
from jax.experimental import pallas as pl
from jax.experimental.pallas import tpu as pltpu
from jax.sharding import PartitionSpec as P

MESH = pl.DeviceIdType.MESH
ROWS, COLS, C, H, HD = 16, 32, 128, 4, 32
NZ, NX, NY, NC = 8, 4, 4, 2
JC = 4
F32, BF16 = jnp.float32, jnp.bfloat16


def device(core, z, yh, x, yl):
    return ((yh * NZ + z) * NC + core, yl * NX + x)


def remote(src, dst, send, recv, where):
    return pltpu.make_async_remote_copy(
        src_ref=src, dst_ref=dst, send_sem=send, recv_sem=recv, device_id=where, device_id_type=MESH
    )


def dot(a, b):
    return jnp.dot(a, b, preferred_element_type=F32)


def dot_nt(a, b):
    return lax.dot_general(a, b, (((1,), (1,)), ((), ())), preferred_element_type=F32)


def kernel(
    pair_ref, gain_ref, shift_ref, wq_ref, wk_ref, wv_ref, wb_ref, wg_ref, gs_ref, wo_ref,
    out_ref,
    ln_ref, norm_ref, part_ref, x_ref, tile_ref, b_ref, k_ref, vt_ref, q_ref, g_ref, upd_ref,
    z_send, z_recv, y_send, y_recv, c_send, c_recv, b_send, b_recv, x_send, x_recv, o_send, o_recv,
):
    blk, col = lax.axis_index("blk"), lax.axis_index("col")
    core, z, yh = lax.rem(blk, NC), lax.rem(blk // NC, NZ), blk // (NC * NZ)
    x, yl = lax.rem(col, NX), col // NX
    other = 1 - core
    bias_yl = yh * NC + core
    to_yh, to_core = yl // NC, lax.rem(yl, NC)
    bias_self = bias_yl == yl
    out_self = core == z // 4

    barrier = pltpu.get_barrier_semaphore()

    def greet(where):
        pl.semaphore_signal(barrier, inc=1, device_id=where, device_id_type=MESH)

    for s in range(NC * 2 * NZ):
        c_s, z_s, yh_s = s % 2, (s // 2) % NZ, s // 16
        mine = bias_self & (c_s == core) & (z_s == z) & (yh_s == yh)

        @pl.when(jnp.logical_not(mine))
        def _():
            greet(device(c_s, z_s, yh_s, x, bias_yl))

    for dz in range(1, NZ):
        greet(device(core, lax.rem(z + dz, NZ), yh, x, yl))
    greet(device(core, z, 1 - yh, x, yl))
    greet(device(other, z, yh, x, yl))
    for dx in range(1, NX):
        greet(device(core, z, yh, lax.rem(x + dx, NX), yl))
    for z_s in range(NZ):
        mine = out_self & (z_s == z)

        @pl.when(jnp.logical_not(mine))
        def _():
            greet(device(z // 4, z_s, yh, x, yl))

    wb = wb_ref[...].astype(F32)
    head = lax.broadcasted_iota(jnp.int32, (C, C), 1) // HD
    wide = jnp.zeros((C, C), F32)
    for h in range(H):
        wide = jnp.where(head == h, wb[:, h : h + 1], wide)
    wide = wide.astype(BF16)
    diagonal = (
        lax.broadcasted_iota(jnp.int32, (COLS, C), 0)
        == lax.broadcasted_iota(jnp.int32, (COLS, C), 1) % HD
    )
    gain, shift = gain_ref[...], shift_ref[...]
    for r in range(0, ROWS, 4):
        v = pair_ref[r : r + 4].reshape(4 * COLS, C).astype(F32)
        v = v - jnp.mean(v, axis=-1, keepdims=True)
        var = jnp.mean(v * v, axis=-1, keepdims=True)
        n = (v * lax.rsqrt(var + 1e-05) * gain + shift).astype(BF16)
        ln_ref[r * COLS : (r + 4) * COLS, :] = n.astype(F32)
        t = dot(n, wide).reshape(4, COLS, C)
        norm_ref[r : r + 4, :] = jnp.sum(jnp.where(diagonal[None], t, 0.0), axis=1)
    tile_ref[...] = norm_ref[...].astype(BF16)
    for j in range(COLS):
        part_ref[j // JC, j % JC] = ln_ref[pl.ds(j, ROWS, stride=COLS), :].astype(BF16)

    sends_bias = 32 - bias_self.astype(jnp.int32)
    sends_out = 8 - out_self.astype(jnp.int32)
    pl.semaphore_wait(barrier, sends_bias + sends_out + 12)

    for dz in range(NZ):
        for dy in range(NY):
            z_d, yl_d = lax.rem(z + dz, NZ), lax.rem(yl + dy, NY)
            dst = b_ref.at[x, yh, core, z]
            cp = remote(tile_ref, dst, b_send, b_recv.at[yh], device(to_core, z_d, to_yh, x, yl_d))
            if dz or dy:
                cp.start()
            else:

                @pl.when(bias_self)
                def _():
                    pltpu.make_async_copy(tile_ref, dst, b_recv.at[yh]).start()

                @pl.when(jnp.logical_not(bias_self))
                def _():
                    cp.start()

    x_ref[yh, core, z] = part_ref[z]
    for dz in range(1, NZ):
        z_d = lax.rem(z + dz, NZ)
        remote(
            part_ref.at[z_d], x_ref.at[yh, core, z], z_send, z_recv, device(core, z_d, yh, x, yl)
        ).start()
    seven = x_ref.at[0, 0, pl.ds(0, NZ - 1)]
    pltpu.make_async_copy(seven, seven, z_recv).wait()

    here = x_ref.at[yh, core]
    cp_y = remote(here, here, y_send, y_recv, device(core, z, 1 - yh, x, yl))
    cp_y.start()
    cp_c0 = remote(here, here, c_send.at[0], c_recv.at[0], device(other, z, yh, x, yl))
    cp_c0.start()

    cp_x = []
    for half in range(2):
        got = b_ref.at[x, half]
        pltpu.make_async_copy(got, got, b_recv.at[half]).wait()
        for dx in range(1, NX):
            cp = remote(
                got, got, x_send.at[half, dx - 1], x_recv.at[half, dx - 1],
                device(core, z, yh, lax.rem(x + dx, NX), yl),
            )
            cp.start()
            cp_x.append(cp)

    wk = wk_ref[...]
    wvt = wv_ref[...].astype(F32).T.astype(BF16)

    def project(half, c):
        rows = x_ref[half, c].reshape(NZ * JC * ROWS, C)
        k_ref[half, c] = dot(rows, wk).astype(BF16).reshape(NZ, JC, ROWS, C)
        for j in range(JC):
            vt_ref[j, half, c] = dot_nt(wvt, x_ref[half, c, :, j].reshape(NZ * ROWS, C)).astype(BF16)

    project(yh, core)
    cp_c0.wait_recv()
    project(yh, other)

    for s in range(NX):
        rows = x_ref[yh, :, core * 4 + s].reshape(NC * JC * ROWS, C)
        q = (dot(rows, wq_ref[...]) * (1.0 / HD**0.5)).astype(BF16)
        q_ref[s] = q.reshape(NC, JC, ROWS, C)
        g_ref[s] = jax.nn.sigmoid(dot(rows, wg_ref[...]) + gs_ref[...]).reshape(NC, JC, ROWS, C)

    cp_y.wait_recv()
    there = x_ref.at[1 - yh, core]
    cp_c1 = remote(there, there, c_send.at[1], c_recv.at[1], device(other, z, yh, x, yl))
    cp_c1.start()
    project(1 - yh, core)
    cp_c1.wait_recv()
    project(1 - yh, other)

    row_head = lax.broadcasted_iota(jnp.int32, (C, C), 0) // HD
    own_head = row_head == head
    lane_head = lax.broadcasted_iota(jnp.int32, (HD, C), 1) // HD

    for dx in range(NX):
        s = lax.rem(x + NX - dx, NX)
        if dx:
            for half in range(2):
                got = b_ref.at[s, half]
                pltpu.make_async_copy(got, got, x_recv.at[half, dx - 1]).wait()
        bias = b_ref.at[s]
        hidden = []
        for j in range(JC):
            q = q_ref[s, :, j].reshape(NC * ROWS, C)
            q = jnp.where(own_head, jnp.concatenate([q] * H, axis=0), jnp.zeros((), BF16))
            k = k_ref[:, :, :, j].reshape(512, C)
            scores = dot_nt(k, q) + bias[...].reshape(512, C).astype(F32)
            expo = jnp.exp(scores - jnp.max(scores, axis=0, keepdims=True))
            total = jnp.sum(expo, axis=0, keepdims=True)
            expo = expo.astype(BF16)
            acc = jnp.zeros((C, C), F32)
            for p in range(4):
                acc = acc + dot(vt_ref[j, p // 2, p % 2], expo[p * 128 : (p + 1) * 128])
            acc = (acc * (1.0 / total)).T
            att = jnp.zeros((HD, C), F32)
            for h in range(H):
                att = jnp.where(lane_head == h, acc[h * HD : (h + 1) * HD], att)
            hidden.append((g_ref[s, :, j].reshape(NC * ROWS, C) * att).astype(BF16))
        hidden = jnp.stack([v.reshape(NC, ROWS, C) for v in hidden], axis=1)
        update = dot(hidden.reshape(NC * JC * ROWS, C), wo_ref[...]).astype(BF16)
        upd_ref[s] = update.reshape(NC, JC, ROWS, C)
        z_d = core * 4 + s
        for c_d in range(NC):
            mine = (z_d == z) & (core == c_d)
            src, dst = upd_ref.at[s, c_d], out_ref.at[z]

            @pl.when(mine)
            def _():
                pltpu.make_async_copy(src, dst, o_recv).start()

            @pl.when(jnp.logical_not(mine))
            def _():
                remote(src, dst, o_send, o_recv, device(c_d, z_d, yh, x, yl)).start()

    pltpu.make_async_copy(out_ref, out_ref, o_recv).wait()
    cp_y.wait_send()
    cp_c0.wait_send()
    cp_c1.wait_send()
    for cp in cp_x:
        cp.wait_send()
    pltpu.make_async_copy(seven, seven, z_send).wait()
    pieces = x_ref.at[0, 0]

    @pl.when(out_self)
    def _():
        pltpu.make_async_copy(seven, seven, o_send).wait()

    @pl.when(jnp.logical_not(out_self))
    def _():
        pltpu.make_async_copy(pieces, pieces, o_send).wait()

    tiles = b_ref.at[0].reshape(32, ROWS, C)

    @pl.when(bias_self)
    def _():
        got = tiles.at[pl.ds(0, 31)]
        pltpu.make_async_copy(got, got, b_send).wait()

    @pl.when(jnp.logical_not(bias_self))
    def _():
        pltpu.make_async_copy(tiles, tiles, b_send).wait()


def per_device(
    pair_rep, norm_gain, norm_shift, w_query, w_key, w_value, w_bias, w_gate, gate_shift, w_out
):
    vmem = pl.BlockSpec(memory_space=pltpu.VMEM)
    dma = pltpu.SemaphoreType.DMA
    result = pl.pallas_call(
        kernel,
        out_shape=jax.ShapeDtypeStruct((NZ, JC, ROWS, C), BF16),
        in_specs=[vmem] * 10,
        out_specs=vmem,
        scratch_shapes=[
            pltpu.VMEM((ROWS * COLS, C), F32),
            pltpu.VMEM((ROWS, C), F32),
            pltpu.VMEM((NZ, JC, ROWS, C), BF16),
            pltpu.VMEM((2, NC, NZ, JC, ROWS, C), BF16),
            pltpu.VMEM((ROWS, C), BF16),
            pltpu.VMEM((NX, 2, NC, NZ, ROWS, C), BF16),
            pltpu.VMEM((2, NC, NZ, JC, ROWS, C), BF16),
            pltpu.VMEM((JC, 2, NC, C, NZ * ROWS), BF16),
            pltpu.VMEM((NX, NC, JC, ROWS, C), BF16),
            pltpu.VMEM((NX, NC, JC, ROWS, C), F32),
            pltpu.VMEM((NX, NC, JC, ROWS, C), BF16),
            dma, dma, dma, dma, dma((2,)), dma((2,)), dma, dma((2,)),
            dma((2, NX - 1)), dma((2, NX - 1)), dma, dma,
        ],
        compiler_params=pltpu.CompilerParams(
            collective_id=0, has_side_effects=True, vmem_limit_bytes=32 << 20
        ),
        name="triangle",
    )(
        pair_rep, norm_gain.reshape(1, C), norm_shift.reshape(1, C), w_query, w_key, w_value,
        w_bias, w_gate, gate_shift.reshape(1, C), w_out,
    )
    return result.reshape(COLS, ROWS, C).transpose(1, 0, 2)


def solution(mesh):
    placed = (P("blk", "col", None),) + (P(),) * 9
    return jax.shard_map(
        per_device, mesh=mesh, in_specs=placed, out_specs=P("blk", "col", None), check_vma=False
    )
```

time: 364 us -> 46.4 us (0.13)
  the two profiles are of different devices: /device:TPU:2 before, /device:TPU:23 now
where the time goes in v1:
time: 46.4 us; the launch traced here: 45.9 us
  Pallas kernels  40.4 us (87%)
  local copies, waits for them, and re-layouts  5.49 us (12%)
    pallas_call x1, Pallas kernels, per_device(): pl.pallas_call(kernel, out_shape=jax.ShapeDtypeStruct((NZ, JC, ROWS, C),...  40.4 us
    unnamed x19, local copies, waits for them, and re-layouts  4.8 us

profile of v1, /device:TPU:23, one launch (start us, length us, event | category | flops | bytes accessed | tf_op | source)
XLA Modules:
  0.0 45.9 jit_solution(10453230270106389635)
XLA Ops:
  0.0 0.0 copy-start.1
  0.0 0.0 copy-start.6
  0.0 0.0 copy-start.7
  0.0 0.0 copy-start.8
  0.0 0.9 %copy.11.wb_ref = bf16[128,4]{1,0:T(8,128)(2,1)S(1)} copy(bf16[128,4]{0,1:T(4,128)(2,1)} %param.16) | data formatting | bytes 2048 | tf_op args[6]
  0.9 0.0 copy-done.1
  0.9 0.0 copy-done.6
  0.9 0.0 copy-done.7
  0.9 0.0 copy-done.8
  0.9 0.0 copy-start
  0.9 0.9 %copy-done = bf16[16,32,128]{2,1,0:T(8,128)(2,1)S(1)} copy-done((bf16[16,32,128]{2,1,0:T(8,128)(2,1)S(1)}, bf16[16,32,128]{2,1,0:T(8,128)(2,1)}, u32[]{:S(2)}) %copy-start) | copy-done | bytes 131096
  1.8 0.0 copy-start.2
  1.8 0.8 %copy-done.2 = bf16[128,128]{1,0:T(8,128)(2,1)S(1)} copy-done((bf16[128,128]{1,0:T(8,128)(2,1)S(1)}, bf16[128,128]{1,0:T(8,128)(2,1)}, u32[]{:S(2)}) %copy-start.2) | copy-done | bytes 32792
  2.6 0.0 copy-start.3
  2.6 0.8 %copy-done.3 = bf16[128,128]{1,0:T(8,128)(2,1)S(1)} copy-done((bf16[128,128]{1,0:T(8,128)(2,1)S(1)}, bf16[128,128]{1,0:T(8,128)(2,1)}, u32[]{:S(2)}) %copy-start.3) | copy-done | bytes 32792
  3.3 0.0 copy-start.4
  3.3 0.8 %copy-done.4 = bf16[128,128]{1,0:T(8,128)(2,1)S(1)} copy-done((bf16[128,128]{1,0:T(8,128)(2,1)S(1)}, bf16[128,128]{1,0:T(8,128)(2,1)}, u32[]{:S(2)}) %copy-start.4) | copy-done | bytes 32792
  4.1 0.0 copy-start.5
  4.1 0.8 %copy-done.5 = bf16[128,128]{1,0:T(8,128)(2,1)S(1)} copy-done((bf16[128,128]{1,0:T(8,128)(2,1)S(1)}, bf16[128,128]{1,0:T(8,128)(2,1)}, u32[]{:S(2)}) %copy-start.5) | copy-done | bytes 32792
  4.8 40.4 %triangle.1 = bf16[8,4,16,128]{3,2,1,0:T(8,128)(2,1)S(1)} custom-call(bf16[16,32,128]{2,1,0:T(8,128)(2,1)S(1)} %copy-done, f32[1,128]{1,0:T(1,128)S(1)} %bitcast.8, f32[1,128]{1,0:T(1,128)S(1)} %bitcast.9, bf16[128,128]{1,0:T(8,128)(2,1)S(1)} %copy-done.1, bf16[128,128]{1,0:T(8,128)(2,1)S(1)} %copy-done.2, bf16[128,128]{1,0:T(8,128)(2,1)S(1)} %copy-done.3, ...), custom_call_target="tpu_custom_call" | custom-call | tf_op jit(solution)/shard_map/triangle/pallas_call | solution.py:250
  45.3 0.7 %copy.14 = bf16[32,16,128]{2,0,1:T(8,128)(2,1)} copy(bf16[32,16,128]{2,1,0:T(8,128)(2,1)S(1)} %bitcast.7) | data formatting | bytes 262144 | tf_op jit(solution)/shard_map/reshape | solution.py:278
Async XLA Ops:
  0.0 0.9 %copy-start.1 = (bf16[128,128]{1,0:T(8,128)(2,1)S(1)}, bf16[128,128]{1,0:T(8,128)(2,1)}, u32[]{:S(2)}) copy-start(bf16[128,128]{1,0:T(8,128)(2,1)} %wq_ref.1) | copy-start | bytes 98308
  0.0 0.9 %copy-start.6 = (f32[128]{0:T(128)S(1)}, f32[128]{0:T(128)}, u32[]{:S(2)}) copy-start(f32[128]{0:T(128)} %param.11) | copy-start | bytes 1540
  0.0 0.9 %copy-start.7 = (f32[128]{0:T(128)S(1)}, f32[128]{0:T(128)}, u32[]{:S(2)}) copy-start(f32[128]{0:T(128)} %param.12) | copy-start | bytes 1540
  0.0 0.9 %copy-start.8 = (f32[128]{0:T(128)S(1)}, f32[128]{0:T(128)}, u32[]{:S(2)}) copy-start(f32[128]{0:T(128)} %param.18) | copy-start | bytes 1540
  0.9 0.9 %copy-start = (bf16[16,32,128]{2,1,0:T(8,128)(2,1)S(1)}, bf16[16,32,128]{2,1,0:T(8,128)(2,1)}, u32[]{:S(2)}) copy-start(bf16[16,32,128]{2,1,0:T(8,128)(2,1)} %pair_ref.1) | copy-start | bytes 393220
  1.8 0.8 %copy-start.2 = (bf16[128,128]{1,0:T(8,128)(2,1)S(1)}, bf16[128,128]{1,0:T(8,128)(2,1)}, u32[]{:S(2)}) copy-start(bf16[128,128]{1,0:T(8,128)(2,1)} %wk_ref.1) | copy-start | bytes 98308
  2.6 0.8 %copy-start.3 = (bf16[128,128]{1,0:T(8,128)(2,1)S(1)}, bf16[128,128]{1,0:T(8,128)(2,1)}, u32[]{:S(2)}) copy-start(bf16[128,128]{1,0:T(8,128)(2,1)} %wv_ref.1) | copy-start | bytes 98308
  3.3 0.8 %copy-start.4 = (bf16[128,128]{1,0:T(8,128)(2,1)S(1)}, bf16[128,128]{1,0:T(8,128)(2,1)}, u32[]{:S(2)}) copy-start(bf16[128,128]{1,0:T(8,128)(2,1)} %wg_ref.1) | copy-start | bytes 98308
  4.1 0.8 %copy-start.5 = (bf16[128,128]{1,0:T(8,128)(2,1)S(1)}, bf16[128,128]{1,0:T(8,128)(2,1)}, u32[]{:S(2)}) copy-start(bf16[128,128]{1,0:T(8,128)(2,1)} %wo_ref.1) | copy-start | bytes 98308

commit v2 on v1

v2 whole, which is shorter than its diff:
```python
import jax
import jax.numpy as jnp
from jax import lax
from jax.experimental import pallas as pl
from jax.experimental.pallas import tpu as pltpu
from jax.sharding import PartitionSpec as P

MESH = pl.DeviceIdType.MESH
ROWS, COLS, C, H, HD = 16, 32, 128, 4, 32
NZ, NX, NY, NC = 8, 4, 4, 2
FAR = (4, 3, 5, 2, 6, 1, 7, 0)
NEAR = (0, 1, 7, 2, 6, 3, 5, 4)
JC = 4
F32, BF16 = jnp.float32, jnp.bfloat16


def device(core, z, yh, x, yl):
    return ((yh * NZ + z) * NC + core, yl * NX + x)


def remote(src, dst, send, recv, where):
    return pltpu.make_async_remote_copy(
        src_ref=src, dst_ref=dst, send_sem=send, recv_sem=recv, device_id=where, device_id_type=MESH
    )


def dot(a, b):
    return jnp.dot(a, b, preferred_element_type=F32)


def dot_nt(a, b):
    return lax.dot_general(a, b, (((1,), (1,)), ((), ())), preferred_element_type=F32)


def kernel(
    pair_hbm, gain_hbm, shift_hbm, wq_hbm, wk_hbm, wv_hbm, wb_hbm, wg_hbm, gs_hbm, wo_hbm,
    out_ref,
    pair_ref, gain_ref, shift_ref, wq_ref, wk_ref, wv_ref, wb_ref, wg_ref, gs_ref, wo_ref,
    ln_ref, norm_ref, part_ref, x_ref, tile_ref, b_ref, k_ref, vt_ref, q_ref, g_ref, upd_ref,
    in_sem, pair_sem,
    n_send, n_recv, c_send, c_recv, b_send, b_recv, x_send, x_recv, o_send, o_recv,
):
    loads = []
    for r in range(4):
        rows = pl.ds(r * 4, 4)
        loads.append(pltpu.make_async_copy(pair_hbm.at[rows], pair_ref.at[rows], pair_sem.at[r]))
    for i, (src, dst) in enumerate((
        (gain_hbm, gain_ref), (shift_hbm, shift_ref), (wb_hbm, wb_ref), (wk_hbm, wk_ref),
        (wv_hbm, wv_ref), (wq_hbm, wq_ref), (wg_hbm, wg_ref), (gs_hbm, gs_ref), (wo_hbm, wo_ref),
    )):
        loads.append(pltpu.make_async_copy(src, dst, in_sem.at[i]))
    for cp in loads:
        cp.start()
    blk, col = lax.axis_index("blk"), lax.axis_index("col")
    core, z, yh = lax.rem(blk, NC), lax.rem(blk // NC, NZ), blk // (NC * NZ)
    x, yl = lax.rem(col, NX), col // NX
    other = 1 - core
    bias_yl = yh * NC + core
    to_yh, to_core = yl // NC, lax.rem(yl, NC)
    bias_self = bias_yl == yl
    out_self = core == z // 4

    barrier = pltpu.get_barrier_semaphore()

    def greet(where):
        pl.semaphore_signal(barrier, inc=1, device_id=where, device_id_type=MESH)

    def unless(condition, action):
        pl.when(jnp.logical_not(condition))(action)

    for dz in FAR:
        z_s = lax.rem(z + dz, NZ)
        for yh_s in range(2):
            for c_s in range(NC):
                mine = bias_self & (c_s == core) & (yh_s == yh) & (dz == 0)
                unless(mine, lambda: greet(device(c_s, z_s, yh_s, x, bias_yl)))
        if dz:
            greet(device(core, z_s, yh, x, yl))
        greet(device(core, z_s, 1 - yh, x, yl))
        unless(out_self & (dz == 0), lambda: greet(device(z // 4, z_s, yh, x, yl)))
    for dx in range(1, NX):
        greet(device(core, z, yh, lax.rem(x + dx, NX), yl))
    greet(device(other, z, yh, x, yl))

    for cp in loads[4:7]:
        cp.wait()
    wide = jnp.concatenate([jnp.broadcast_to(wb_ref[h : h + 1].astype(F32), (HD, C)) for h in range(H)])
    wide = wide.astype(BF16)
    diagonal = (
        lax.broadcasted_iota(jnp.int32, (COLS, C), 0)
        == lax.broadcasted_iota(jnp.int32, (COLS, C), 1) % HD
    )
    gain, shift = gain_ref[...], shift_ref[...]
    for r in range(0, ROWS, 4):
        loads[r // 4].wait()
        v = pair_ref[r : r + 4].reshape(4 * COLS, C).astype(F32)
        v = v - jnp.mean(v, axis=-1, keepdims=True)
        var = jnp.mean(v * v, axis=-1, keepdims=True)
        n = (v * lax.rsqrt(var + 1e-05) * gain + shift).astype(BF16)
        ln_ref[r * COLS : (r + 4) * COLS, :] = n.astype(F32)
        t = dot_nt(n, wide).reshape(4, COLS, C)
        norm_ref[r : r + 4, :] = jnp.sum(jnp.where(diagonal[None], t, 0.0), axis=1)
    tile_ref[...] = norm_ref[...].astype(BF16)
    for j in range(COLS):
        part_ref[j // JC, j % JC] = ln_ref[pl.ds(j, ROWS, stride=COLS), :].astype(BF16)

    sends_bias = 32 - bias_self.astype(jnp.int32)
    sends_out = 8 - out_self.astype(jnp.int32)
    pl.semaphore_wait(barrier, sends_bias + sends_out + 19)

    for dz in FAR:
        z_d = lax.rem(z + dz, NZ)
        tile_dst = b_ref.at[x, yh, z, core]
        for dy in (2, 1, 3, 0):
            yl_d = lax.rem(yl + dy, NY)
            cp = remote(tile_ref, tile_dst, b_send, b_recv.at[z], device(to_core, z_d, to_yh, x, yl_d))
            if dz or dy:
                cp.start()
            else:
                pl.when(bias_self)(
                    lambda: pltpu.make_async_copy(tile_ref, tile_dst, b_recv.at[z]).start()
                )
                unless(bias_self, cp.start)
    for dz in FAR:
        z_d = lax.rem(z + dz, NZ)
        for yh_d in (1 - yh, yh):
            if dz or yh_d is not yh:
                remote(
                    part_ref.at[z_d], x_ref.at[yh, z, core], n_send, n_recv.at[yh, z],
                    device(core, z_d, yh_d, x, yl),
                ).start()
            else:
                pltpu.make_async_copy(part_ref.at[z], x_ref.at[yh, z, core], n_recv.at[yh, z]).start()

    def arrived(ref, sem):
        pltpu.make_async_copy(ref, ref, sem).wait()

    for cp in loads[7:]:
        cp.wait()
    wk = wk_ref[...]
    wvt = wv_ref[...].astype(F32).T.astype(BF16)

    for dz in NEAR:
        z_s = lax.rem(z + dz, NZ)
        got = b_ref.at[x, :, z_s]
        arrived(got, b_recv.at[z_s])
        for dx in (2, 1, 3):
            remote(
                got, got, x_send, x_recv.at[dx - 1], device(core, z, yh, lax.rem(x + dx, NX), yl)
            ).start()
    def share(half):
        for dz in NEAR:
            z_s = lax.rem(z + dz, NZ)
            here = x_ref.at[half, z_s, core]
            arrived(here, n_recv.at[half, z_s])
            remote(here, here, c_send, c_recv.at[half, z_s], device(other, z, yh, x, yl)).start()

    def project(half, four):
        for z_s in range(4):
            z_s = four * 4 + z_s
            arrived(x_ref.at[half, z_s, other], c_recv.at[half, z_s])
        part = x_ref.at[half, pl.ds(four * 4, 4)]
        rows = part[...].reshape(8 * JC * ROWS, C)
        k_ref[half, pl.ds(four * 4, 4)] = dot(rows, wk).astype(BF16).reshape(4, NC, JC, ROWS, C)
        for j in range(JC):
            vt_ref[j, half, four] = dot_nt(wvt, part[:, :, j].reshape(8 * ROWS, C)).astype(BF16)

    share(yh)
    project(yh, z // 4)
    project(yh, 1 - z // 4)

    for s in range(NX):
        rows = x_ref[yh, core * 4 + s].reshape(NC * JC * ROWS, C)
        q = (dot(rows, wq_ref[...]) * (1.0 / HD**0.5)).astype(BF16)
        q_ref[s] = q.reshape(NC, JC, ROWS, C)
        g_ref[s] = jax.nn.sigmoid(dot(rows, wg_ref[...]) + gs_ref[...]).reshape(NC, JC, ROWS, C)

    share(1 - yh)
    project(1 - yh, z // 4)
    project(1 - yh, 1 - z // 4)

    own_head = (
        lax.broadcasted_iota(jnp.int32, (C, C), 0) // HD
        == lax.broadcasted_iota(jnp.int32, (C, C), 1) // HD
    )
    lane_head = lax.broadcasted_iota(jnp.int32, (HD, C), 1) // HD

    for dx in (0, 1, 3, 2):
        s = lax.rem(x + NX - dx, NX)
        bias = b_ref.at[s]
        if dx:
            arrived(bias, x_recv.at[dx - 1])
        hidden = []
        for j in range(JC):
            q = q_ref[s, :, j].reshape(NC * ROWS, C)
            q = jnp.where(own_head, jnp.concatenate([q] * H, axis=0), jnp.zeros((), BF16))
            k = k_ref[:, :, :, j].reshape(512, C)
            scores = dot_nt(k, q) + bias[...].reshape(512, C).astype(F32)
            expo = jnp.exp(scores - jnp.max(scores, axis=0, keepdims=True))
            total = jnp.sum(expo, axis=0, keepdims=True)
            expo = expo.astype(BF16)
            acc = jnp.zeros((C, C), F32)
            for p in range(4):
                acc = acc + dot(vt_ref[j, p // 2, p % 2], expo[p * 128 : (p + 1) * 128])
            acc = (acc * (1.0 / total)).T
            att = jnp.zeros((HD, C), F32)
            for h in range(H):
                att = jnp.where(lane_head == h, acc[h * HD : (h + 1) * HD], att)
            hidden.append((g_ref[s, :, j].reshape(NC * ROWS, C) * att).astype(BF16))
        hidden = jnp.stack([v.reshape(NC, ROWS, C) for v in hidden], axis=1)
        update = dot(hidden.reshape(NC * JC * ROWS, C), wo_ref[...]).astype(BF16)
        upd_ref[s] = update.reshape(NC, JC, ROWS, C)
        z_d = core * 4 + s
        for c_d in range(NC):
            mine = (z_d == z) & (core == c_d)
            src, dst = upd_ref.at[s, c_d], out_ref.at[z]
            pl.when(mine)(lambda: pltpu.make_async_copy(src, dst, o_recv).start())
            unless(mine, remote(src, dst, o_send, o_recv, device(c_d, z_d, yh, x, yl)).start)

    arrived(out_ref, o_recv)
    pieces = x_ref.reshape(NZ * 2 * NC, JC, ROWS, C)
    tiles = b_ref.reshape(NX * 32, ROWS, C)
    arrived(pieces.at[pl.ds(0, 15)], n_send)
    arrived(pieces.at[pl.ds(0, 16)], c_send)
    arrived(b_ref.at[pl.ds(0, 3)], x_send)
    pl.when(out_self)(lambda: arrived(pieces.at[pl.ds(0, 7)], o_send))
    unless(out_self, lambda: arrived(pieces.at[pl.ds(0, 8)], o_send))
    pl.when(bias_self)(lambda: arrived(tiles.at[pl.ds(0, 31)], b_send))
    unless(bias_self, lambda: arrived(tiles.at[pl.ds(0, 32)], b_send))


def per_device(
    pair_rep, norm_gain, norm_shift, w_query, w_key, w_value, w_bias, w_gate, gate_shift, w_out
):
    dma = pltpu.SemaphoreType.DMA
    result = pl.pallas_call(
        kernel,
        out_shape=jax.ShapeDtypeStruct((NZ, JC, ROWS, C), BF16),
        in_specs=[pl.BlockSpec(memory_space=pltpu.HBM)] * 10,
        out_specs=pl.BlockSpec(memory_space=pltpu.VMEM),
        scratch_shapes=[
            pltpu.VMEM((ROWS, COLS, C), BF16),
            pltpu.VMEM((1, C), F32),
            pltpu.VMEM((1, C), F32),
            pltpu.VMEM((C, C), BF16),
            pltpu.VMEM((C, C), BF16),
            pltpu.VMEM((C, C), BF16),
            pltpu.VMEM((H, C), BF16),
            pltpu.VMEM((C, C), BF16),
            pltpu.VMEM((1, C), F32),
            pltpu.VMEM((C, C), BF16),
            pltpu.VMEM((ROWS * COLS, C), F32),
            pltpu.VMEM((ROWS, C), F32),
            pltpu.VMEM((NZ, JC, ROWS, C), BF16),
            pltpu.VMEM((2, NZ, NC, JC, ROWS, C), BF16),
            pltpu.VMEM((ROWS, C), BF16),
            pltpu.VMEM((NX, 2, NZ, NC, ROWS, C), BF16),
            pltpu.VMEM((2, NZ, NC, JC, ROWS, C), BF16),
            pltpu.VMEM((JC, 2, 2, C, 8 * ROWS), BF16),
            pltpu.VMEM((NX, NC, JC, ROWS, C), BF16),
            pltpu.VMEM((NX, NC, JC, ROWS, C), F32),
            pltpu.VMEM((NX, NC, JC, ROWS, C), BF16),
            dma((9,)), dma((4,)),
            dma, dma((2, NZ)), dma, dma((2, NZ)),
            dma, dma((NZ,)), dma, dma((NX - 1,)), dma, dma,
        ],
        compiler_params=pltpu.CompilerParams(
            collective_id=0, has_side_effects=True, vmem_limit_bytes=32 << 20
        ),
        name="triangle",
    )(*(
        pltpu.with_memory_space_constraint(v, pltpu.HBM)
        for v in (
            pair_rep, norm_gain.reshape(1, C), norm_shift.reshape(1, C), w_query, w_key, w_value,
            w_bias.T, w_gate, gate_shift.reshape(1, C), w_out,
        )
    ))
    return result.reshape(COLS, ROWS, C).transpose(1, 0, 2)


def solution(mesh):
    placed = (P("blk", "col", None),) + (P(),) * 9
    return jax.shard_map(
        per_device, mesh=mesh, in_specs=placed, out_specs=P("blk", "col", None), check_vma=False
    )
```

time: 46.4 us -> 40.8 us (0.88)
  the two profiles are of different devices: /device:TPU:23 before, /device:TPU:73 now
where the time goes in v2:
time: 40.8 us; the launch traced here: 40.6 us
  Pallas kernels  39.9 us (98%)
  local copies, waits for them, and re-layouts  0.69 us (2%)
    pallas_call x1, Pallas kernels, per_device(): pl.pallas_call(kernel, out_shape=jax.ShapeDtypeStruct((NZ, JC, ROWS, C),...  39.9 us

profile of v2, /device:TPU:73, one launch (start us, length us, event | category | flops | bytes accessed | tf_op | source)
XLA Modules:
  0.0 40.6 jit_solution(8549738059116850290)
XLA Ops:
  0.0 39.9 %triangle.1 = bf16[8,4,16,128]{3,2,1,0:T(8,128)(2,1)S(1)} custom-call(bf16[16,32,128]{2,1,0:T(8,128)(2,1)} %pair_hbm.1, f32[1,128]{1,0:T(1,128)} %bitcast.10, f32[1,128]{1,0:T(1,128)} %bitcast.11, bf16[128,128]{1,0:T(8,128)(2,1)} %wq_hbm.1, bf16[128,128]{1,0:T(8,128)(2,1)} %wk_hbm.1, bf16[128,128]{1,0:T(8,128)(2,1)} %wv_hbm.1, bf16[4,128]{1,0:T(4,128)(2,1)} %bitcast.9, ...), custom_call_target="tpu_custom_call" | custom-call | tf_op jit(solution)/shard_map/triangle/pallas_call | solution.py:236
  40.0 0.7 %copy.13 = bf16[32,16,128]{2,0,1:T(8,128)(2,1)} copy(bf16[32,16,128]{2,1,0:T(8,128)(2,1)S(1)} %bitcast.8) | data formatting | bytes 262144 | tf_op jit(solution)/shard_map/reshape | solution.py:278

commit v3 on v2

--- a/solution.py
+++ b/solution.py
@@ -38,7 +38,7 @@
     pair_ref, gain_ref, shift_ref, wq_ref, wk_ref, wv_ref, wb_ref, wg_ref, gs_ref, wo_ref,
     ln_ref, norm_ref, part_ref, x_ref, tile_ref, b_ref, k_ref, vt_ref, q_ref, g_ref, upd_ref,
     in_sem, pair_sem,
-    n_send, n_recv, c_send, c_recv, b_send, b_recv, x_send, x_recv, o_send, o_recv,
+    t_send, t_recv, n_send, n_recv, y_send, y_recv, c_send, c_recv, b_send, b_recv, x_send, x_recv, o_send, o_recv,
 ):
     loads = []
     for r in range(4):
@@ -49,7 +49,7 @@
         (wv_hbm, wv_ref), (wq_hbm, wq_ref), (wg_hbm, wg_ref), (gs_hbm, gs_ref), (wo_hbm, wo_ref),
     )):
         loads.append(pltpu.make_async_copy(src, dst, in_sem.at[i]))
-    for cp in loads:
+    for cp in loads[:7]:
         cp.start()
     blk, col = lax.axis_index("blk"), lax.axis_index("col")
     core, z, yh = lax.rem(blk, NC), lax.rem(blk // NC, NZ), blk // (NC * NZ)
@@ -70,17 +70,20 @@
 
     for dz in FAR:
         z_s = lax.rem(z + dz, NZ)
-        for yh_s in range(2):
-            for c_s in range(NC):
-                mine = bias_self & (c_s == core) & (yh_s == yh) & (dz == 0)
-                unless(mine, lambda: greet(device(c_s, z_s, yh_s, x, bias_yl)))
         if dz:
             greet(device(core, z_s, yh, x, yl))
-        greet(device(core, z_s, 1 - yh, x, yl))
         unless(out_self & (dz == 0), lambda: greet(device(z // 4, z_s, yh, x, yl)))
+    for yh_s in range(2):
+        for c_s in range(NC):
+            mine = bias_self & (c_s == core) & (yh_s == yh)
+            unless(mine, lambda: greet(device(c_s, z, yh_s, x, bias_yl)))
+    greet(device(core, z, 1 - yh, x, yl))
     for dx in range(1, NX):
         greet(device(core, z, yh, lax.rem(x + dx, NX), yl))
     greet(device(other, z, yh, x, yl))
+
+    for cp in loads[7:]:
+        cp.start()
 
     for cp in loads[4:7]:
         cp.wait()
@@ -101,59 +104,78 @@
         t = dot_nt(n, wide).reshape(4, COLS, C)
         norm_ref[r : r + 4, :] = jnp.sum(jnp.where(diagonal[None], t, 0.0), axis=1)
     tile_ref[...] = norm_ref[...].astype(BF16)
+
     for j in range(COLS):
         part_ref[j // JC, j % JC] = ln_ref[pl.ds(j, ROWS, stride=COLS), :].astype(BF16)
 
-    sends_bias = 32 - bias_self.astype(jnp.int32)
+    sends_bias = 4 - bias_self.astype(jnp.int32)
     sends_out = 8 - out_self.astype(jnp.int32)
-    pl.semaphore_wait(barrier, sends_bias + sends_out + 19)
+    pl.semaphore_wait(barrier, sends_bias + sends_out + 12)
 
     for dz in FAR:
         z_d = lax.rem(z + dz, NZ)
-        tile_dst = b_ref.at[x, yh, z, core]
-        for dy in (2, 1, 3, 0):
-            yl_d = lax.rem(yl + dy, NY)
-            cp = remote(tile_ref, tile_dst, b_send, b_recv.at[z], device(to_core, z_d, to_yh, x, yl_d))
-            if dz or dy:
-                cp.start()
-            else:
-                pl.when(bias_self)(
-                    lambda: pltpu.make_async_copy(tile_ref, tile_dst, b_recv.at[z]).start()
-                )
-                unless(bias_self, cp.start)
-    for dz in FAR:
-        z_d = lax.rem(z + dz, NZ)
-        for yh_d in (1 - yh, yh):
-            if dz or yh_d is not yh:
-                remote(
-                    part_ref.at[z_d], x_ref.at[yh, z, core], n_send, n_recv.at[yh, z],
-                    device(core, z_d, yh_d, x, yl),
-                ).start()
-            else:
-                pltpu.make_async_copy(part_ref.at[z], x_ref.at[yh, z, core], n_recv.at[yh, z]).start()
+        if dz:
+            remote(
+                part_ref.at[z_d], x_ref.at[yh, z, core], n_send, n_recv.at[z],
+                device(core, z_d, yh, x, yl),
+            ).start()
+        else:
+            pltpu.make_async_copy(part_ref.at[z], x_ref.at[yh, z, core], n_recv.at[z]).start()
+
+    tile_dst = b_ref.at[x, yh, z, core]
+    for dy in (2, 1, 3, 0):
+        yl_d = lax.rem(yl + dy, NY)
+        cp = remote(tile_ref, tile_dst, t_send, t_recv, device(to_core, z, to_yh, x, yl_d))
+        if dy:
+            cp.start()
+        else:
+            pl.when(bias_self)(lambda: pltpu.make_async_copy(tile_ref, tile_dst, t_recv).start())
+            unless(bias_self, cp.start)
 
     def arrived(ref, sem):
         pltpu.make_async_copy(ref, ref, sem).wait()
+
+    def share(dz):
+        z_s = lax.rem(z + dz, NZ)
+        here = x_ref.at[yh, z_s, core]
+        arrived(here, n_recv.at[z_s])
+        remote(here, here, y_send, y_recv.at[z_s], device(core, z, 1 - yh, x, yl)).start()
+        remote(here, here, c_send, c_recv.at[yh, z_s], device(other, z, yh, x, yl)).start()
+
+    def spread(dz):
+        z_s = lax.rem(z + dz, NZ)
+        got = b_ref.at[x, :, z_s]
+        if dz:
+            arrived(got, b_recv.at[z_s])
+        for dx in (2, 1, 3):
+            remote(
+                got, got, x_send, x_recv.at[dx - 1], device(core, z, yh, lax.rem(x + dx, NX), yl)
+            ).start()
+
+    def share_other():
+        for dz in NEAR:
+            z_s = lax.rem(z + dz, NZ)
+            there = x_ref.at[1 - yh, z_s, core]
+            arrived(there, y_recv.at[z_s])
+            remote(there, there, c_send, c_recv.at[1 - yh, z_s], device(other, z, yh, x, yl)).start()
+
+    share(0)
+    own_z = b_ref.at[x, :, z]
+    arrived(own_z, t_recv)
+    for dz in FAR[:-1]:
+        remote(
+            own_z, own_z, b_send, b_recv.at[z], device(core, lax.rem(z + dz, NZ), yh, x, yl)
+        ).start()
+    spread(0)
+    for dz in NEAR[1:]:
+        share(dz)
+    for dz in NEAR[1:]:
+        spread(dz)
 
     for cp in loads[7:]:
         cp.wait()
     wk = wk_ref[...]
     wvt = wv_ref[...].astype(F32).T.astype(BF16)
-
-    for dz in NEAR:
-        z_s = lax.rem(z + dz, NZ)
-        got = b_ref.at[x, :, z_s]
-        arrived(got, b_recv.at[z_s])
-        for dx in (2, 1, 3):
-            remote(
-                got, got, x_send, x_recv.at[dx - 1], device(core, z, yh, lax.rem(x + dx, NX), yl)
-            ).start()
-    def share(half):
-        for dz in NEAR:
-            z_s = lax.rem(z + dz, NZ)
-            here = x_ref.at[half, z_s, core]
-            arrived(here, n_recv.at[half, z_s])
-            remote(here, here, c_send, c_recv.at[half, z_s], device(other, z, yh, x, yl)).start()
 
     def project(half, four):
         for z_s in range(4):
@@ -165,7 +187,6 @@
         for j in range(JC):
             vt_ref[j, half, four] = dot_nt(wvt, part[:, :, j].reshape(8 * ROWS, C)).astype(BF16)
 
-    share(yh)
     project(yh, z // 4)
     project(yh, 1 - z // 4)
 
@@ -175,7 +196,7 @@
         q_ref[s] = q.reshape(NC, JC, ROWS, C)
         g_ref[s] = jax.nn.sigmoid(dot(rows, wg_ref[...]) + gs_ref[...]).reshape(NC, JC, ROWS, C)
 
-    share(1 - yh)
+    share_other()
     project(1 - yh, z // 4)
     project(1 - yh, 1 - z // 4)
 
@@ -220,13 +241,15 @@
     arrived(out_ref, o_recv)
     pieces = x_ref.reshape(NZ * 2 * NC, JC, ROWS, C)
     tiles = b_ref.reshape(NX * 32, ROWS, C)
-    arrived(pieces.at[pl.ds(0, 15)], n_send)
+    arrived(pieces.at[pl.ds(0, 7)], n_send)
+    arrived(pieces.at[pl.ds(0, 8)], y_send)
     arrived(pieces.at[pl.ds(0, 16)], c_send)
     arrived(b_ref.at[pl.ds(0, 3)], x_send)
     pl.when(out_self)(lambda: arrived(pieces.at[pl.ds(0, 7)], o_send))
     unless(out_self, lambda: arrived(pieces.at[pl.ds(0, 8)], o_send))
-    pl.when(bias_self)(lambda: arrived(tiles.at[pl.ds(0, 31)], b_send))
-    unless(bias_self, lambda: arrived(tiles.at[pl.ds(0, 32)], b_send))
+    arrived(tiles.at[pl.ds(0, 28)], b_send)
+    pl.when(bias_self)(lambda: arrived(tiles.at[pl.ds(0, 3)], t_send))
+    unless(bias_self, lambda: arrived(tiles.at[pl.ds(0, 4)], t_send))
 
 
 def per_device(
@@ -261,7 +284,7 @@
             pltpu.VMEM((NX, NC, JC, ROWS, C), F32),
             pltpu.VMEM((NX, NC, JC, ROWS, C), BF16),
             dma((9,)), dma((4,)),
-            dma, dma((2, NZ)), dma, dma((2, NZ)),
+            dma, dma, dma, dma((NZ,)), dma, dma((NZ,)), dma, dma((2, NZ)),
             dma, dma((NZ,)), dma, dma((NX - 1,)), dma, dma,
         ],
         compiler_params=pltpu.CompilerParams(

time: 40.8 us -> 37.4 us (0.917)
  the two profiles are of different devices: /device:TPU:73 before, /device:TPU:5 now
where the time goes in v3:
time: 37.4 us; the launch traced here: 37.2 us
  Pallas kernels  36.5 us (98%)
  local copies, waits for them, and re-layouts  0.69 us (2%)
    pallas_call x1, Pallas kernels, per_device(): pl.pallas_call(kernel, out_shape=jax.ShapeDtypeStruct((NZ, JC, ROWS, C),...  36.5 us

profile of v3, /device:TPU:5, one launch (start us, length us, event | category | flops | bytes accessed | tf_op | source)
XLA Modules:
  0.0 37.2 jit_solution(8038897782120586737)
XLA Ops:
  0.0 36.5 %triangle.1 = bf16[8,4,16,128]{3,2,1,0:T(8,128)(2,1)S(1)} custom-call(bf16[16,32,128]{2,1,0:T(8,128)(2,1)} %pair_hbm.1, f32[1,128]{1,0:T(1,128)} %bitcast.10, f32[1,128]{1,0:T(1,128)} %bitcast.11, bf16[128,128]{1,0:T(8,128)(2,1)} %wq_hbm.1, bf16[128,128]{1,0:T(8,128)(2,1)} %wk_hbm.1, bf16[128,128]{1,0:T(8,128)(2,1)} %wv_hbm.1, bf16[4,128]{1,0:T(4,128)(2,1)} %bitcast.9, ...), custom_call_target="tpu_custom_call" | custom-call | tf_op jit(solution)/shard_map/triangle/pallas_call | solution.py:259
  36.5 0.7 %copy.13 = bf16[32,16,128]{2,0,1:T(8,128)(2,1)} copy(bf16[32,16,128]{2,1,0:T(8,128)(2,1)S(1)} %bitcast.8) | data formatting | bytes 262144 | tf_op jit(solution)/shard_map/reshape | solution.py:301

commit v4 on v3

--- a/solution.py
+++ b/solution.py
@@ -82,8 +82,6 @@
         greet(device(core, z, yh, lax.rem(x + dx, NX), yl))
     greet(device(other, z, yh, x, yl))
 
-    for cp in loads[7:]:
-        cp.start()
 
     for cp in loads[4:7]:
         cp.wait()
@@ -94,15 +92,16 @@
         == lax.broadcasted_iota(jnp.int32, (COLS, C), 1) % HD
     )
     gain, shift = gain_ref[...], shift_ref[...]
-    for r in range(0, ROWS, 4):
-        loads[r // 4].wait()
-        v = pair_ref[r : r + 4].reshape(4 * COLS, C).astype(F32)
+    for r in range(0, ROWS, 16):
+        for cp in loads[r // 4 : (r + 16) // 4]:
+            cp.wait()
+        v = pair_ref[r : r + 16].reshape(16 * COLS, C).astype(F32)
         v = v - jnp.mean(v, axis=-1, keepdims=True)
         var = jnp.mean(v * v, axis=-1, keepdims=True)
         n = (v * lax.rsqrt(var + 1e-05) * gain + shift).astype(BF16)
-        ln_ref[r * COLS : (r + 4) * COLS, :] = n.astype(F32)
-        t = dot_nt(n, wide).reshape(4, COLS, C)
-        norm_ref[r : r + 4, :] = jnp.sum(jnp.where(diagonal[None], t, 0.0), axis=1)
+        ln_ref[r * COLS : (r + 16) * COLS, :] = n.astype(F32)
+        t = dot_nt(n, wide).reshape(16, COLS, C)
+        norm_ref[r : r + 16, :] = jnp.sum(jnp.where(diagonal[None], t, 0.0), axis=1)
     tile_ref[...] = norm_ref[...].astype(BF16)
 
     for j in range(COLS):
@@ -121,6 +120,9 @@
             ).start()
         else:
             pltpu.make_async_copy(part_ref.at[z], x_ref.at[yh, z, core], n_recv.at[z]).start()
+
+    for cp in loads[7:]:
+        cp.start()
 
     tile_dst = b_ref.at[x, yh, z, core]
     for dy in (2, 1, 3, 0):
@@ -206,10 +208,17 @@
     )
     lane_head = lax.broadcasted_iota(jnp.int32, (HD, C), 1) // HD
 
-    for dx in (0, 1, 3, 2):
+    def way(dx):
+        steps = lax.rem(core * 4 + lax.rem(x + NX - dx, NX) - z + NZ, NZ)
+        return jnp.minimum(steps, NZ - steps)
+
+    one, two, three = way(1), way(2), way(3)
+    last = jnp.where((one <= two) & (one <= three), 1, jnp.where(three <= two, 3, 2))
+    turns = (0, jnp.where(last == 1, 3, 1), jnp.where(last == 2, 3, 2), last)
+    for turn, dx in enumerate(turns):
         s = lax.rem(x + NX - dx, NX)
         bias = b_ref.at[s]
-        if dx:
+        if turn:
             arrived(bias, x_recv.at[dx - 1])
         hidden = []
         for j in range(JC):

time: 37.4 us -> 36.8 us (0.984)
  the two profiles are of different devices: /device:TPU:5 before, /device:TPU:13 now
where the time goes in v4:
time: 36.8 us; the launch traced here: 36.6 us
  Pallas kernels  35.9 us (98%)
  local copies, waits for them, and re-layouts  0.69 us (2%)
    pallas_call x1, Pallas kernels, per_device(): pl.pallas_call(kernel, out_shape=jax.ShapeDtypeStruct((NZ, JC, ROWS, C),...  35.9 us

profile of v4, /device:TPU:13, one launch (start us, length us, event | category | flops | bytes accessed | tf_op | source)
XLA Modules:
  0.0 36.6 jit_solution(3326866641909988753)
XLA Ops:
  0.0 35.9 %triangle.1 = bf16[8,4,16,128]{3,2,1,0:T(8,128)(2,1)S(1)} custom-call(bf16[16,32,128]{2,1,0:T(8,128)(2,1)} %pair_hbm.1, f32[1,128]{1,0:T(1,128)} %bitcast.10, f32[1,128]{1,0:T(1,128)} %bitcast.11, bf16[128,128]{1,0:T(8,128)(2,1)} %wq_hbm.1, bf16[128,128]{1,0:T(8,128)(2,1)} %wk_hbm.1, bf16[128,128]{1,0:T(8,128)(2,1)} %wv_hbm.1, bf16[4,128]{1,0:T(4,128)(2,1)} %bitcast.9, ...), custom_call_target="tpu_custom_call" | custom-call | tf_op jit(solution)/shard_map/triangle/pallas_call | solution.py:268
  35.9 0.7 %copy.13 = bf16[32,16,128]{2,0,1:T(8,128)(2,1)} copy(bf16[32,16,128]{2,1,0:T(8,128)(2,1)S(1)} %bitcast.8) | data formatting | bytes 262144 | tf_op jit(solution)/shard_map/reshape | solution.py:310

commit v5 on v4

--- a/solution.py
+++ b/solution.py
@@ -38,7 +38,7 @@
     pair_ref, gain_ref, shift_ref, wq_ref, wk_ref, wv_ref, wb_ref, wg_ref, gs_ref, wo_ref,
     ln_ref, norm_ref, part_ref, x_ref, tile_ref, b_ref, k_ref, vt_ref, q_ref, g_ref, upd_ref,
     in_sem, pair_sem,
-    t_send, t_recv, n_send, n_recv, y_send, y_recv, c_send, c_recv, b_send, b_recv, x_send, x_recv, o_send, o_recv,
+    t_send, t_recv, n_send, n_recv, y_send, y_recv, c_send, h_recv, c_recv, b_send, b_recv, x_send, x_recv, o_send, o_recv,
 ):
     loads = []
     for r in range(4):
@@ -142,7 +142,6 @@
         here = x_ref.at[yh, z_s, core]
         arrived(here, n_recv.at[z_s])
         remote(here, here, y_send, y_recv.at[z_s], device(core, z, 1 - yh, x, yl)).start()
-        remote(here, here, c_send, c_recv.at[yh, z_s], device(other, z, yh, x, yl)).start()
 
     def spread(dz):
         z_s = lax.rem(z + dz, NZ)
@@ -159,7 +158,7 @@
             z_s = lax.rem(z + dz, NZ)
             there = x_ref.at[1 - yh, z_s, core]
             arrived(there, y_recv.at[z_s])
-            remote(there, there, c_send, c_recv.at[1 - yh, z_s], device(other, z, yh, x, yl)).start()
+            remote(there, there, c_send, c_recv.at[z_s], device(other, z, yh, x, yl)).start()
 
     share(0)
     own_z = b_ref.at[x, :, z]
@@ -171,6 +170,8 @@
     spread(0)
     for dz in NEAR[1:]:
         share(dz)
+    mine = x_ref.at[yh, :, core]
+    remote(mine, mine, c_send, h_recv, device(other, z, yh, x, yl)).start()
     for dz in NEAR[1:]:
         spread(dz)
 
@@ -180,17 +181,20 @@
     wvt = wv_ref[...].astype(F32).T.astype(BF16)
 
     def project(half, four):
-        for z_s in range(4):
-            z_s = four * 4 + z_s
-            arrived(x_ref.at[half, z_s, other], c_recv.at[half, z_s])
+        if half is not yh:
+            for z_s in range(4):
+                z_s = four * 4 + z_s
+                arrived(x_ref.at[half, z_s, other], c_recv.at[z_s])
         part = x_ref.at[half, pl.ds(four * 4, 4)]
         rows = part[...].reshape(8 * JC * ROWS, C)
         k_ref[half, pl.ds(four * 4, 4)] = dot(rows, wk).astype(BF16).reshape(4, NC, JC, ROWS, C)
         for j in range(JC):
             vt_ref[j, half, four] = dot_nt(wvt, part[:, :, j].reshape(8 * ROWS, C)).astype(BF16)
 
+    arrived(x_ref.at[yh, :, other], h_recv)
     project(yh, z // 4)
     project(yh, 1 - z // 4)
+    share_other()
 
     for s in range(NX):
         rows = x_ref[yh, core * 4 + s].reshape(NC * JC * ROWS, C)
@@ -198,7 +202,6 @@
         q_ref[s] = q.reshape(NC, JC, ROWS, C)
         g_ref[s] = jax.nn.sigmoid(dot(rows, wg_ref[...]) + gs_ref[...]).reshape(NC, JC, ROWS, C)
 
-    share_other()
     project(1 - yh, z // 4)
     project(1 - yh, 1 - z // 4)
 
@@ -293,7 +296,7 @@
             pltpu.VMEM((NX, NC, JC, ROWS, C), F32),
             pltpu.VMEM((NX, NC, JC, ROWS, C), BF16),
             dma((9,)), dma((4,)),
-            dma, dma, dma, dma((NZ,)), dma, dma((NZ,)), dma, dma((2, NZ)),
+            dma, dma, dma, dma((NZ,)), dma, dma((NZ,)), dma, dma, dma((NZ,)),
             dma, dma((NZ,)), dma, dma((NX - 1,)), dma, dma,
         ],
         compiler_params=pltpu.CompilerParams(

time: 36.8 us -> 36.7 us (level)
  no operation moved by 1% of the time
where the time goes in v5:
time: 36.7 us; the launch traced here: 36.5 us
  Pallas kernels  35.8 us (98%)
  local copies, waits for them, and re-layouts  0.69 us (2%)
    pallas_call x1, Pallas kernels, per_device(): pl.pallas_call(kernel, out_shape=jax.ShapeDtypeStruct((NZ, JC, ROWS, C),...  35.8 us

profile of v5, /device:TPU:13, one launch (start us, length us, event | category | flops | bytes accessed | tf_op | source)
XLA Modules:
  0.0 36.5 jit_solution(12497932079575955375)
XLA Ops:
  0.0 35.8 %triangle.1 = bf16[8,4,16,128]{3,2,1,0:T(8,128)(2,1)S(1)} custom-call(bf16[16,32,128]{2,1,0:T(8,128)(2,1)} %pair_hbm.1, f32[1,128]{1,0:T(1,128)} %bitcast.10, f32[1,128]{1,0:T(1,128)} %bitcast.11, bf16[128,128]{1,0:T(8,128)(2,1)} %wq_hbm.1, bf16[128,128]{1,0:T(8,128)(2,1)} %wk_hbm.1, bf16[128,128]{1,0:T(8,128)(2,1)} %wv_hbm.1, bf16[4,128]{1,0:T(4,128)(2,1)} %bitcast.9, ...), custom_call_target="tpu_custom_call" | custom-call | tf_op jit(solution)/shard_map/triangle/pallas_call | solution.py:271
  35.8 0.7 %copy.13 = bf16[32,16,128]{2,0,1:T(8,128)(2,1)} copy(bf16[32,16,128]{2,1,0:T(8,128)(2,1)S(1)} %bitcast.8) | data formatting | bytes 262144 | tf_op jit(solution)/shard_map/reshape | solution.py:313

commit v6 on v5

--- a/solution.py
+++ b/solution.py
@@ -194,21 +194,25 @@
     arrived(x_ref.at[yh, :, other], h_recv)
     project(yh, z // 4)
     project(yh, 1 - z // 4)
-    share_other()
-
-    for s in range(NX):
-        rows = x_ref[yh, core * 4 + s].reshape(NC * JC * ROWS, C)
-        q = (dot(rows, wq_ref[...]) * (1.0 / HD**0.5)).astype(BF16)
-        q_ref[s] = q.reshape(NC, JC, ROWS, C)
-        g_ref[s] = jax.nn.sigmoid(dot(rows, wg_ref[...]) + gs_ref[...]).reshape(NC, JC, ROWS, C)
-
-    project(1 - yh, z // 4)
-    project(1 - yh, 1 - z // 4)
-
     own_head = (
         lax.broadcasted_iota(jnp.int32, (C, C), 0) // HD
         == lax.broadcasted_iota(jnp.int32, (C, C), 1) // HD
     )
+    wqt = wq_ref[...].astype(F32).T.astype(BF16)
+    for s in range(NX):
+        block = x_ref.at[yh, core * 4 + s]
+        for j in range(JC):
+            rows = block[:, j].reshape(NC * ROWS, C)
+            q = dot_nt(wqt, jnp.concatenate([rows] * H, axis=0)) * (1.0 / HD**0.5)
+            q_ref[s, j] = jnp.where(own_head, q, 0.0).astype(BF16)
+        gate = jax.nn.sigmoid(dot(block[...].reshape(NC * JC * ROWS, C), wg_ref[...]) + gs_ref[...])
+        g_ref[s] = gate.reshape(NC, JC, ROWS, C)
+
+    share_other()
+
+    project(1 - yh, z // 4)
+    project(1 - yh, 1 - z // 4)
+
     lane_head = lax.broadcasted_iota(jnp.int32, (HD, C), 1) // HD
 
     def way(dx):
@@ -225,10 +229,8 @@
             arrived(bias, x_recv.at[dx - 1])
         hidden = []
         for j in range(JC):
-            q = q_ref[s, :, j].reshape(NC * ROWS, C)
-            q = jnp.where(own_head, jnp.concatenate([q] * H, axis=0), jnp.zeros((), BF16))
             k = k_ref[:, :, :, j].reshape(512, C)
-            scores = dot_nt(k, q) + bias[...].reshape(512, C).astype(F32)
+            scores = dot(k, q_ref[s, j]) + bias[...].reshape(512, C).astype(F32)
             expo = jnp.exp(scores - jnp.max(scores, axis=0, keepdims=True))
             total = jnp.sum(expo, axis=0, keepdims=True)
             expo = expo.astype(BF16)
@@ -292,7 +294,7 @@
             pltpu.VMEM((NX, 2, NZ, NC, ROWS, C), BF16),
             pltpu.VMEM((2, NZ, NC, JC, ROWS, C), BF16),
             pltpu.VMEM((JC, 2, 2, C, 8 * ROWS), BF16),
-            pltpu.VMEM((NX, NC, JC, ROWS, C), BF16),
+            pltpu.VMEM((NX, JC, C, C), BF16),
             pltpu.VMEM((NX, NC, JC, ROWS, C), F32),
             pltpu.VMEM((NX, NC, JC, ROWS, C), BF16),
             dma((9,)), dma((4,)),

time: 36.7 us -> 36.7 us (level)
  no operation moved by 1% of the time
where the time goes in v6:
time: 36.7 us; the launch traced here: 36.5 us
  Pallas kernels  35.8 us (98%)
  local copies, waits for them, and re-layouts  0.69 us (2%)
    pallas_call x1, Pallas kernels, per_device(): pl.pallas_call(kernel, out_shape=jax.ShapeDtypeStruct((NZ, JC, ROWS, C),...  35.8 us

profile of v6, /device:TPU:13, one launch (start us, length us, event | category | flops | bytes accessed | tf_op | source)
XLA Modules:
  0.0 36.5 jit_solution(762326894252063276)
XLA Ops:
  0.0 35.8 %triangle.1 = bf16[8,4,16,128]{3,2,1,0:T(8,128)(2,1)S(1)} custom-call(bf16[16,32,128]{2,1,0:T(8,128)(2,1)} %pair_hbm.1, f32[1,128]{1,0:T(1,128)} %bitcast.10, f32[1,128]{1,0:T(1,128)} %bitcast.11, bf16[128,128]{1,0:T(8,128)(2,1)} %wq_hbm.1, bf16[128,128]{1,0:T(8,128)(2,1)} %wk_hbm.1, bf16[128,128]{1,0:T(8,128)(2,1)} %wv_hbm.1, bf16[4,128]{1,0:T(4,128)(2,1)} %bitcast.9, ...), custom_call_target="tpu_custom_call" | custom-call | tf_op jit(solution)/shard_map/triangle/pallas_call | solution.py:273
  35.8 0.7 %copy.13 = bf16[32,16,128]{2,0,1:T(8,128)(2,1)} copy(bf16[32,16,128]{2,1,0:T(8,128)(2,1)S(1)} %bitcast.8) | data formatting | bytes 262144 | tf_op jit(solution)/shard_map/reshape | solution.py:315
